TPU v7x, 128 devices: a whole 4x4x4 slice. The times are simulated.
128 devices in a mesh: fsdp: 4 (over z), seq: 8 (over x, core), tensor: 4 (over y).
Axes of the slice: x: 4, y: 4, z: 4, core: 2. Of those that a mesh axis runs over, the one named last changes fastest.
Arguments:
- block_input: bfloat16 [16384, 512], P(('fsdp', 'seq', 'tensor')), may hold values from -6 to 6
- cotangent: bfloat16 [16384, 512], P(('fsdp', 'seq', 'tensor')), may hold values from -6 to 6
- doc_lengths: int32 [4, 4], P('fsdp'), may hold values from 1 to 3840, as said below
- joint_weight: float32 [512, 1536], P(('fsdp', 'seq', 'tensor')), may hold values from -0.375 to 0.375
- output_weight: float32 [512, 512], P(('fsdp', 'seq', 'tensor')), may hold values from -1.5 to 1.5
- expand_weight: float32 [512, 2048], P(('fsdp', 'seq', 'tensor')), may hold values from -0.25 to 0.25
- reduce_weight: float32 [512, 2048], P(('fsdp', 'seq', 'tensor')), may hold values from -0.125 to 0.125
- joint_moment: float32 [512, 1536], P(('fsdp', 'seq', 'tensor')), may hold values from -4096 to 4096
- output_moment: float32 [512, 512], P(('fsdp', 'seq', 'tensor')), may hold values from -224 to 224
- expand_moment: float32 [512, 2048], P(('fsdp', 'seq', 'tensor')), may hold values from -224 to 224
- reduce_moment: float32 [512, 2048], P(('fsdp', 'seq', 'tensor')), may hold values from -448 to 448
- vectors: float32 [11, 512], P(None, ('fsdp', 'seq', 'tensor'))
- first_moment: float32 [11, 512], P(None, ('fsdp', 'seq', 'tensor'))
- second_moment: float32 [11, 512], P(None, ('fsdp', 'seq', 'tensor'))
Outputs:
- block_output: bfloat16 [16384, 512], P(('fsdp', 'seq', 'tensor'))
- input_grad: float32 [16384, 512], P(('fsdp', 'seq', 'tensor'))
- gradient_joint: float32 [512, 1536], P(('fsdp', 'seq', 'tensor'))
- gradient_output: float32 [512, 512], P(('fsdp', 'seq', 'tensor'))
- gradient_expand: float32 [512, 2048], P(('fsdp', 'seq', 'tensor'))
- gradient_reduce: float32 [512, 2048], P(('fsdp', 'seq', 'tensor'))
- momentum_joint: float32 [512, 1536], P(('fsdp', 'seq', 'tensor'))
- momentum_output: float32 [512, 512], P(('fsdp', 'seq', 'tensor'))
- momentum_expand: float32 [512, 2048], P(('fsdp', 'seq', 'tensor'))
- momentum_reduce: float32 [512, 2048], P(('fsdp', 'seq', 'tensor'))
- updated_joint: float32 [512, 1536], P(('fsdp', 'seq', 'tensor'))
- updated_output: float32 [512, 512], P(('fsdp', 'seq', 'tensor'))
- updated_expand: float32 [512, 2048], P(('fsdp', 'seq', 'tensor'))
- updated_reduce: float32 [512, 2048], P(('fsdp', 'seq', 'tensor'))
- vector_grad: float32 [11, 512], P(None, ('fsdp', 'seq', 'tensor'))
- second_next: float32 [11, 512], P(None, ('fsdp', 'seq', 'tensor'))
- vector_next: float32 [11, 512], P(None, ('fsdp', 'seq', 'tensor'))
Inputs may be any that keep to these rules, and one draw needn't show every extreme that they name: `doc_lengths`: each row gives the lengths of the 4 documents of one pack in order; they sum to 4096, and exactly one of them, at a place drawn from the seed, is 3840 tokens long.
All inputs are finite; a program needn't handle non-finite values.
Results may differ from a plain program's by a relative error of at most 0.014.
The roundings to bfloat16 on the way count: a program that leaves them out, or rounds other values in their place, can miss the bound.
Values may be sent and summed in bfloat16 or wider, within the bound.
A program may use at most 128 MiB of HBM per device.

v0:
```python
import functools
import math

import jax
import jax.numpy as jnp
from jax import lax
from jax.experimental import pallas as pl
from jax.experimental.pallas import tpu as pltpu
from jax.sharding import PartitionSpec as P

D = 512
HEADS = 8
FF = 2048
ROT = 16
HD = 64
STEP = 10

norm_epsilon = 1e-05
masked_score = -1e30
newton_first = 3.4445
newton_second = -4.775
newton_third = 2.0315
beta_first = 0.9
beta_second = 0.95
adam_epsilon = 1e-08
vector_rate = 0.2
muon_rate = 0.25
muon_beta = 0.95
muon_decay = 0.01
LOG2_E = 1.4426950408889634

BF = jnp.bfloat16
F32 = jnp.float32
MESH = pl.DeviceIdType.MESH
VMEM = pl.BlockSpec(memory_space=pltpu.VMEM)
SMEM = pl.BlockSpec(memory_space=pltpu.SMEM)
ANY = pl.BlockSpec(memory_space=pl.ANY)
WIDTHS = (3 * D, D, FF, FF)


def shape(dims, dtype):
    return jax.ShapeDtypeStruct(dims, dtype)


class Place:
    def __init__(self):
        self.z = lax.axis_index("fsdp")
        self.seq = lax.axis_index("seq")
        self.t = lax.axis_index("tensor")
        self.x = lax.div(self.seq, 2)
        self.c = lax.rem(self.seq, 2)
        self.d = 1 - 2 * self.c
        self.a = self.c * self.x + (1 - self.c) * self.z
        self.b = self.c * self.z + (1 - self.c) * self.x
        self.mate = self.x + 1 - 2 * lax.rem(self.x, 2)
        self.cross = 3 - self.x
        self.head = lax.div(self.x, 2)

    def at(self, z=None, x=None, c=None, t=None):
        z = self.z if z is None else z
        x = self.x if x is None else x
        c = self.c if c is None else c
        t = self.t if t is None else t
        return (z, 2 * x + c, t)

    def at_a(self, a):
        c = self.c
        return self.at(z=(1 - c) * a + c * self.z, x=c * a + (1 - c) * self.x)

    def at_b(self, b):
        c = self.c
        return self.at(z=c * b + (1 - c) * self.z, x=(1 - c) * b + c * self.x)

    def at_ab(self, a, b):
        c = self.c
        return self.at(z=(1 - c) * a + c * b, x=c * a + (1 - c) * b)

    def plane(self):
        steps = [(i, j) for i in range(4) for j in range(4) if i + j > 0]
        steps.sort(key=lambda step: -min(step[0], 4 - step[0]) - min(step[1], 4 - step[1]))
        return [(ring(self.a, i), ring(self.b, j)) for i, j in steps]

    def sibling(self):
        return self.at(c=1 - self.c)

    def octet(self):
        g = 4 * self.c + self.t
        members = [lax.rem(g + k, 8) for k in range(1, 8)]
        return [self.at(c=lax.div(m, 4), t=lax.rem(m, 4)) for m in members]

    def row_x(self):
        return [self.at(x=lax.rem(self.x + k, 4)) for k in range(1, 4)]

    def row_z(self):
        return [self.at(z=lax.rem(self.z + k, 4)) for k in range(1, 4)]

    def row_t(self):
        return [self.at(t=lax.rem(self.t + k, 4)) for k in range(1, 4)]


def ring(index, step):
    return lax.rem(index + step + 4, 4)


def greet(partners):
    barrier = pltpu.get_barrier_semaphore()
    for partner in partners:
        pl.semaphore_signal(barrier, inc=1, device_id=partner, device_id_type=MESH)
    return lambda: pl.semaphore_wait(barrier, len(partners))


class Wire:
    def __init__(self, send, recv, local):
        self.send = send
        self.recv = recv
        self.local = local
        self.count = 0
        self.loads = 0
        self.open = []

    def push(self, src, dst, device):
        index = self.count
        self.count += 1
        copy = pltpu.make_async_remote_copy(
            src_ref=src,
            dst_ref=dst,
            send_sem=self.send.at[index],
            recv_sem=self.recv.at[index],
            device_id=device,
            device_id_type=MESH,
        )
        copy.start()
        self.open.append(copy)
        return copy

    def offer(self, first, source, target, sender, goal, device):
        return pltpu.make_async_remote_copy(
            src_ref=source,
            dst_ref=target,
            send_sem=self.send.at[first + goal],
            recv_sem=self.recv.at[first + sender],
            device_id=device,
            device_id_type=MESH,
        )

    def block(self, count):
        first = self.count
        self.count += count
        return first

    def load(self, src, dst):
        copy = pltpu.make_async_copy(src, dst, self.local.at[self.loads])
        self.loads += 1
        copy.start()
        return copy

    def drain(self):
        for copy in self.open:
            copy.wait_send()
        self.open = []


def arrive(copies):
    for copy in copies:
        copy.wait_recv()


def dot(left, right):
    return jnp.dot(left, right, preferred_element_type=F32)


def dot_cols(left, right):
    return lax.dot_general(left, right, (((1,), (1,)), ((), ())), preferred_element_type=F32)


def dot_rows(left, right):
    return lax.dot_general(left, right, (((0,), (0,)), ((), ())), preferred_element_type=F32)


def turn(values, cosine, sine, sign):
    lane = lax.rem(lax.broadcasted_iota(jnp.int32, values.shape, 1), 64)
    crossed = jnp.where(lane < 8, -pltpu.roll(values, 120, 1), pltpu.roll(values, 8, 1))
    return values * cosine + crossed * (sine * sign)


def vec_row(v_ref, row):
    return jnp.concatenate([v_ref[k, row : row + 1, :] for k in range(4)], axis=1)


def normalise(rows):
    wide = rows.astype(F32)
    centred = wide - jnp.mean(wide, axis=-1, keepdims=True)
    variance = jnp.mean(centred * centred, axis=-1, keepdims=True)
    rate = lax.rsqrt(variance + norm_epsilon)
    return centred * rate, rate


def halves(values):
    high = values.astype(BF)
    return high, (values - high.astype(F32)).astype(BF)


def product(left_h, left_l, right_h, right_l):
    return dot(left_h, right_h) + (dot(left_h, right_l) + dot(left_l, right_h))


def squared(high, small):
    cross = dot(high, small)
    return dot(high, high) + (cross + cross.T)


def spread_b(wire, place, ref):
    block = ref.at[place.c, place.a, place.b]
    return [wire.push(block, block, place.at_b(ring(place.b, k))) for k in range(1, 4)]


class Ring:
    def __init__(self, wire, place, ref, index, at):
        self.wire = wire
        self.place = place
        self.ref = ref
        self.index = index
        self.at = at
        self.ups, self.downs = {}, {}
        for p, q in ((0, 2), (1, 3), (2, 0), (3, 1)):
            self.ups[p] = self.send(0, p, 1)
            self.downs[q] = self.send(0, q, -1)
        self.swaps = [self.swap(0)]

    def send(self, step, part, way):
        block = self.ref.at[self.place.c, ring(self.index, step), part]
        return self.wire.push(block, block, self.at(ring(self.index, way)))

    def swap(self, step):
        block = self.ref.at[self.place.c, ring(self.index, step)]
        return self.wire.push(block, block, self.place.sibling())

    def hand_on(self):
        self.more = []
        for p, q in ((0, 2), (1, 3)):
            self.ups[p].wait_recv()
            self.more.append(self.send(-1, p, 1))
            self.downs[q].wait_recv()
            self.more.append(self.send(1, q, -1))

    def close(self):
        arrive([self.ups[2], self.ups[3]])
        self.swaps.append(self.swap(-1))
        arrive([self.downs[0], self.downs[1]])
        self.swaps.append(self.swap(1))
        arrive(self.more)
        self.swaps.append(self.swap(2))


def spread_plane(wire, place, ref):
    block = ref.at[place.c, place.a, place.b]
    return [wire.push(block, block, place.at_ab(a, b)) for a, b in place.plane()]


def scatter_plane(wire, place, ref, target):
    copies = []
    for k, (a, b) in enumerate(place.plane()):
        copies.append(wire.push(ref.at[a, b], target.at[k], place.at_ab(a, b)))
    return copies


def add_plane(first, parts):
    value = first.astype(F32)
    for k in range(15):
        value = value + parts[k].astype(F32)
    return value


def swap_cores(wire, place, ref):
    return wire.push(ref.at[place.c], ref.at[place.c], place.sibling())


def natural(source, target, start, stop):
    for z in range(4):
        for x in range(4):
            target[8 * z + 2 * x] = source[0, z, x, :, start:stop]
            target[8 * z + 2 * x + 1] = source[1, x, z, :, start:stop]


def by_row(source, target, start, stop):
    for z in range(4):
        for x in range(4):
            for c in range(2):
                target[8 * z + 2 * x + c] = source[c, z, x, :, start:stop]


def by_owner(target, z, rows, start, stop):
    for x in range(4):
        target[0, z, x, :, start:stop] = rows[32 * x : 32 * x + 16, :]
        target[1, x, z, :, start:stop] = rows[32 * x + 16 : 32 * x + 32, :]


def by_core(target, z, rows, start, stop):
    for x in range(4):
        for c in range(2):
            block = rows[32 * x + 16 * c : 32 * x + 16 * c + 16, :]
            target[c, z, x, :, start:stop] = block


def sum_cores(wire, place, ref, target):
    return wire.push(ref.at[1 - place.c], target, place.sibling())


def trade_t(wire, place, source, target):
    copies = []
    for k in range(1, 4):
        goal = ring(place.t, k)
        copies.append(wire.push(source.at[goal], target.at[place.t], place.at(t=goal)))
    return copies


def total(first, parts):
    value = first.astype(F32)
    for k in range(3):
        value = value + parts[k].astype(F32)
    return value


def unpair(target, part, k):
    one, two = part[:, 128:256], part[:, 256:384]
    target[:, 128 * k : 128 * k + 128] = part[:, 0:128]
    target[:, 512 + 128 * k : 640 + 128 * k] = jnp.concatenate(
        [one[:, 0:64], two[:, 0:64]], axis=1
    )
    target[:, 1024 + 128 * k : 1152 + 128 * k] = jnp.concatenate(
        [one[:, 64:128], two[:, 64:128]], axis=1
    )


INPUTS = (
    "lengths",
    "x",
    "c",
    "joint",
    "output",
    "expand",
    "reduce",
    "vectors",
    "m_joint",
    "m_output",
    "m_expand",
    "m_reduce",
    "first",
    "second",
)

OUTPUTS = (
    ("g_joint", (4, 1536), F32),
    ("g_output", (4, 512), F32),
    ("g_expand", (4, 2048), F32),
    ("g_reduce", (4, 2048), F32),
    ("n_joint", (4, 1536), F32),
    ("n_output", (4, 512), F32),
    ("n_expand", (4, 2048), F32),
    ("n_reduce", (4, 2048), F32),
    ("u_joint", (4, 1536), F32),
    ("u_output", (4, 512), F32),
    ("u_expand", (4, 2048), F32),
    ("u_reduce", (4, 2048), F32),
    ("block_output", (128, 512), BF),
    ("input_grad", (128, 512), F32),
    ("vector_grad", (4, 11), F32),
    ("second_next", (4, 11), F32),
    ("vector_next", (4, 11), F32),
)

SCRATCH = (
    ("joint_v", (4, 1536), F32),
    ("output_v", (4, 512), F32),
    ("expand_v", (4, 2048), F32),
    ("reduce_v", (4, 2048), F32),
    ("vectors_v", (4, 11), F32),
    ("first_v", (4, 11), F32),
    ("second_v", (4, 11), F32),
    ("table", (128, 128), F32),
    ("vec_sum", (4, 16, 128), F32),
    ("m_joint_v", (4, 1536), F32),
    ("m_output_v", (4, 512), F32),
    ("m_expand_v", (4, 2048), F32),
    ("m_reduce_v", (4, 2048), F32),
    ("j_out", (4, 4, 384), F32),
    ("j_in", (4, 4, 384), F32),
    ("j_rows", (16, 384), F32),
    ("w_out", (4, 4, 1536), F32),
    ("w_in", (4, 4, 1536), F32),
    ("w_rows", (16, 1536), F32),
    ("wj", (2, 4, 4, 16, 512), BF),
    ("wr", (2, 4, 4, 16, 1536), BF),
    ("w_joint", (32, 16, 384), BF),
    ("w_output", (32, 16, 512), BF),
    ("w_expand", (32, 16, 512), BF),
    ("w_reduce", (32, 16, 512), BF),
    ("v_own", (16, 128), F32),
    ("m_own", (4, 4, 2048), F32),
    ("m_early", (4, 4, 2048), F32),
    ("m_old", (16, 2048), F32),
    ("v_in", (4, 16, 128), F32),
    ("v", (4, 16, 128), F32),
    ("rows_x", (4, 128, 512), BF),
    ("rows_c", (4, 128, 512), BF),
    ("cos", (4, 128, 128), F32),
    ("sin", (4, 128, 128), F32),
    ("normed", (4, 128, 512), BF),
    ("q_turned", (2, 128, 256), BF),
    ("q_buf", (2, 64, 512), BF),
    ("q_heads", (2, 64, 512), BF),
    ("g_buf", (2, 64, 512), BF),
    ("g_heads", (2, 64, 512), BF),
    ("kv_buf", (2, 512, 128), BF),
    ("kv", (8, 512, 128), BF),
    ("hidden", (4, 128, 512), BF),
    ("pre", (4, 128, 512), BF),
    ("feed", (4, 128, 512), F32),
    ("row_grad", (4, 128, 512), F32),
    ("gf", (2, 4, 4, 16, 1024), BF),
    ("gf_core", (4, 4, 16, 1024), BF),
    ("gf_chip", (4, 4, 16, 1024), BF),
    ("gf_z", (3, 4, 16, 1024), BF),
    ("gf_line", (4, 16, 1024), BF),
    ("gf_x", (3, 16, 1024), BF),
    ("go", (2, 4, 4, 16, 128), BF),
    ("go_core", (4, 4, 16, 128), BF),
    ("go_chip", (4, 4, 16, 128), BF),
    ("go_in", (15, 16, 128), BF),
    ("early_out", (4, 4, 1152), F32),
    ("early_in", (4, 4, 1152), F32),
    ("turned", (8, 128, 512), BF),
    ("keys", (8, 512, 128), BF),
    ("scores", (9, 512, 512), F32),
    ("sums", (8, 512, 128), F32),
    ("query_low", (2, 512, 128), BF),
    ("query_two", (2, 512, 128), BF),
    ("begin", (2, 1, 512), jnp.int32),
    ("top", (2, 1, 512), F32),
    ("total_sum", (2, 1, 512), F32),
    ("out_turned", (2, 64, 512), F32),
    ("grad_low", (2, 512, 128), BF),
    ("back_turned", (64, 512), F32),
    ("centre", (2, 1, 512), F32),
    ("out_low", (2, 64, 512), BF),
    ("out_heads", (2, 64, 512), BF),
    ("back_low", (2, 64, 512), BF),
    ("back_heads", (2, 64, 512), BF),
    ("dk", (2, 4, 512, 128), BF),
    ("dk_in", (4, 512, 128), BF),
    ("dk_chip", (4, 512, 128), BF),
    ("dk_got", (3, 512, 128), BF),
    ("dkv", (2, 512, 128), BF),
    ("pair_out", (128, 512), BF),
    ("joint_out", (512, 384), BF),
    ("out_cols", (4, 128, 128), BF),
    ("out_in", (4, 128, 128), BF),
    ("out_part", (4, 128, 512), BF),
    ("out_got", (4, 128, 512), BF),
    ("back_part", (4, 128, 512), BF),
    ("back_got", (4, 128, 512), BF),
    ("gj", (2, 4, 4, 16, 384), BF),
    ("gj_core", (4, 4, 16, 384), BF),
    ("gj_chip", (4, 4, 16, 384), BF),
    ("gj_in", (15, 16, 384), BF),
    ("late_out", (4, 4, 384), F32),
    ("late_in", (4, 4, 384), F32),
    ("vp", (4, 4, 16, 128), F32),
    ("vp_core", (4, 16, 128), F32),
    ("vp_z", (3, 4, 16, 128), F32),
    ("vp_x", (3, 4, 16, 128), F32),
    ("vp_t", (3, 4, 16, 128), F32),
    ("gm_out", (4, 16, 512), BF),
    ("gm_in", (4, 16, 512), BF),
    ("m_rows", (16, 2048), F32),
    ("momentum", (2, 4, 4, 16, 1536), BF),
    ("extra", (2, 4, 4, 16, 512), BF),
    ("gram", (512, 512), F32),
    ("gram_h", (512, 512), BF),
    ("gram_l", (512, 512), BF),
    ("poly_h", (512, 512), BF),
    ("poly_l", (512, 512), BF),
    ("temp_h", (512, 512), BF),
    ("temp_l", (512, 512), BF),
    ("own", (16, 512), F32),
    ("u_rows", (4, 16, 512), F32),
    ("u_out", (4, 16, 512), BF),
    ("u_in", (4, 16, 512), BF),
    ("u_wide", (4, 4, 2048), F32),
)

PUSHES = 240
LOADS = 16


class Box:
    pass


def attend_chunk(place, slot):
    return place.seq if slot == 0 else 7 - place.seq


def attend_score(slot, k):
    return 8 - k if slot == 0 else k


def pairs(count, step, carry):
    def two(k, carry):
        return step(2 * k + 1, step(2 * k, carry))

    def one(_, carry):
        return step(count - 1, carry)

    carry = lax.fori_loop(0, lax.div(count, 2), two, carry)
    return lax.fori_loop(0, lax.rem(count, 2), one, carry)


def attend_start(r, place):
    for slot in range(2):
        index = 512 * attend_chunk(place, slot) + lax.broadcasted_iota(jnp.int32, (1, 512), 1)
        begin = jnp.zeros((1, 512), jnp.int32)
        finish = 0
        for j in range(4):
            finish = finish + r.lengths[0, j]
            begin = jnp.where(index >= finish, finish, begin)
        r.begin[slot] = begin
        r.top[slot] = jnp.full((1, 512), masked_score, F32)
        r.total_sum[slot] = jnp.zeros((1, 512), F32)


def query_prepare(r, slot):
    wide = r.q_heads[slot].astype(F32)
    high, small = halves(wide * (HD ** -0.5 * LOG2_E))
    r.query_two[slot] = jnp.concatenate([high, small], axis=0).T
    low = (wide * (HD ** -0.5)).astype(BF)
    r.query_low[slot] = jnp.concatenate([low, jnp.zeros((64, 512), BF)], axis=0).T


def grad_prepare(r, slot):
    r.grad_low[slot] = jnp.concatenate([jnp.zeros((64, 512), BF), r.g_heads[slot]], axis=0).T


def keys_prepare(r, column):
    low = lax.broadcasted_iota(jnp.int32, (512, 128), 1) < 64
    for part in range(2):
        k = 2 * column + part
        r.turned[k] = r.kv[k].T
        wide = r.kv[k].astype(F32)
        r.keys[k] = jnp.where(low, wide, pltpu.roll(wide, 64, 1)).astype(BF)


def score_column(r, place, column, slot, diagonal=False):
    chunk = attend_chunk(place, slot)

    def run(parts):
        top, total_sum = r.top[slot], r.total_sum[slot]
        for part, last in parts:
            k = 2 * column + part
            raw = dot_cols(r.keys[k], r.query_two[slot])
            key = lax.broadcasted_iota(jnp.int32, (512, 512), 0)
            allowed = key >= r.begin[slot] - 512 * k
            if last:
                allowed = allowed & (key <= lax.broadcasted_iota(jnp.int32, (512, 512), 1))
            raw = jnp.where(allowed, raw, masked_score)
            r.scores[attend_score(slot, k)] = raw
            higher = jnp.maximum(top, jnp.max(raw, axis=0, keepdims=True))
            total_part = jnp.sum(jnp.exp2(raw - higher), axis=0, keepdims=True)
            total_sum = total_sum * jnp.exp2(top - higher) + total_part
            top = higher
        r.top[slot] = top
        r.total_sum[slot] = total_sum

    if not diagonal:

        @pl.when(2 * column + 1 < chunk)
        def _():
            run(((0, False), (1, False)))

        return

    @pl.when(2 * column + 1 == chunk)
    def _():
        run(((0, False), (1, True)))

    @pl.when(2 * column == chunk)
    def _():
        run(((0, True),))


def weigh_values(r, place, slot):
    level = r.top[slot] + jnp.log(r.total_sum[slot]) * LOG2_E

    def weigh(k, out):
        prob = jnp.exp2(r.scores[attend_score(slot, k)] - level)
        r.scores[attend_score(slot, k)] = prob
        return out + dot(r.turned[k, 64:128, :], prob.astype(BF))

    out = pairs(attend_chunk(place, slot) + 1, weigh, jnp.zeros((64, 512), F32))
    r.out_turned[slot] = out
    r.out_low[slot] = out.astype(BF)


def backward_block(r, slot, k):
    prob = r.scores[attend_score(slot, k)]
    out_grad = r.grad_low[slot]
    grad = dot_cols(r.kv[k], out_grad)
    score_grad = (prob * (grad - r.centre[slot])).astype(BF)
    r.sums[k] += dot(prob.astype(BF), out_grad) + dot(score_grad, r.query_low[slot])
    return dot(r.turned[k, 0:64, :], score_grad)


def backward_cross(r, place):
    def step(k, back):
        return back + backward_block(r, 1, k)

    back = pairs(attend_chunk(place, 1) + 1, step, jnp.zeros((64, 512), F32))
    r.back_low[1] = (back * (HD ** -0.5)).astype(BF)


def backward_column(r, place, column, diagonal):
    chunk = attend_chunk(place, 0)

    @pl.when(2 * column + 1 <= chunk)
    def _():
        r.back_turned[...] += backward_block(r, 0, 2 * column) + backward_block(
            r, 0, 2 * column + 1
        )

    if diagonal:

        @pl.when(2 * column == chunk)
        def _():
            r.back_turned[...] += backward_block(r, 0, 2 * column)

    r.dk[0, column] = r.sums[2 * column].astype(BF)
    r.dk[1, column] = r.sums[2 * column + 1].astype(BF)


def newton(r, place):
    blocks, size = 1, 512

    def rows(i):
        return pl.ds(size * i, size)

    def diagonal(i):
        row = size * i + lax.broadcasted_iota(jnp.int32, (size, 512), 0)
        return row == lax.broadcasted_iota(jnp.int32, (size, 512), 1)

    def fill(i, trace):
        value = jnp.zeros((size, 512), F32)
        for k in range(3):
            lanes = slice(512 * k, 512 * k + 512)
            right = r.momentum[:, :, :, :, lanes].reshape(512, 512)
            value = value + dot_cols(right, right)
        r.gram[rows(i), :] = value

        @pl.when(place.t >= 2)
        def _():
            right = r.extra[...].reshape(512, 512)
            r.gram[rows(i), :] += dot_cols(right, right)

        value = r.gram[rows(i), :]
        return trace + jnp.sum(jnp.where(diagonal(i), value, 0.0), keepdims=True)

    trace = lax.fori_loop(0, blocks, fill, jnp.zeros((1, 1), F32))
    scale = 1.0 / (jnp.sqrt(trace) + 1e-07)

    def keep(value, i, high_ref, low_ref):
        high, small = halves(value)
        high_ref[rows(i), :] = high
        low_ref[rows(i), :] = small

    def prepare(i, _):
        value = r.gram[rows(i), :] * (scale * scale)
        r.gram[rows(i), :] = value
        keep(value, i, r.gram_h, r.gram_l)
        return 0

    lax.fori_loop(0, blocks, prepare, 0)

    def polynomial(i, _):
        square = squared(r.gram_h[...], r.gram_l[...])
        value = (
            jnp.where(diagonal(i), newton_first, 0.0)
            + newton_second * r.gram[rows(i), :]
            + newton_third * square
        )
        keep(value, i, r.poly_h, r.poly_l)
        return 0

    def inner(i, _):
        high, small = r.poly_h[...], r.poly_l[...]
        own_h, own_l = halves(r.own[...])
        left = jnp.concatenate([high, own_h], axis=0)
        cross = dot(left, small)
        main = dot(jnp.concatenate([left, own_l], axis=0), high)
        r.own[...] = main[512:528] + (main[528:544] + cross[512:528])
        keep(main[0:512] + (cross[0:512] + cross[0:512].T), i, r.temp_h, r.temp_l)
        return 0

    def outer(i, _):
        value = product(r.gram_h[...], r.gram_l[...], r.temp_h[...], r.temp_l[...])
        r.gram[rows(i), :] = value
        keep(value, i, r.gram_h, r.gram_l)
        return 0

    def times(left, right_h, right_l):
        high, small = halves(left)
        both = dot(jnp.concatenate([high, small], axis=0), right_h[...])
        return both[0:16] + (both[16:32] + dot(high, right_l[...]))

    mine = 256 * place.c + 64 * place.a + 16 * place.b
    row = lax.broadcasted_iota(jnp.int32, (16, 512), 0)
    column = lax.broadcasted_iota(jnp.int32, (16, 512), 1)
    r.own[...] = jnp.where(column - row == mine, 1.0, 0.0)

    def sweep(_, carry):
        polynomial(0, 0)
        inner(0, 0)
        outer(0, 0)
        return carry

    lax.fori_loop(0, 3, sweep, 0)
    lax.fori_loop(0, blocks, polynomial, 0)
    lax.fori_loop(0, blocks, inner, 0)

    def last_gram(left):
        return times(times(left, r.gram_h, r.gram_l), r.temp_h, r.temp_l)

    own = r.own[...]
    once = last_gram(own)
    own = newton_first * own + newton_second * once + newton_third * last_gram(once)
    return halves(own * scale)


def block_kernel(*refs):
    r = Box()
    names = list(INPUTS) + [n for n, _, _ in OUTPUTS] + [n for n, _, _ in SCRATCH]
    for name, ref in zip(names, refs):
        setattr(r, name, ref)
    place = Place()
    wire = Wire(*refs[-3:])
    z, x, c, t, d = place.z, place.x, place.c, place.t, place.d
    seq, mate, cross, head = place.seq, place.mate, place.cross, place.head
    sibling = place.sibling()

    met = greet(
        place.octet()
        + [place.at_ab(a, b) for a, b in place.plane()]
        + [place.at(x=cross, c=1 - c)]
    )

    load_w = [
        wire.load(r.joint, r.joint_v),
        wire.load(r.output, r.output_v),
        wire.load(r.expand, r.expand_v),
        wire.load(r.reduce, r.reduce_v),
    ]
    load_v = wire.load(r.vectors, r.vectors_v)
    load_x = wire.load(r.x, r.rows_x.at[t])
    load_c = wire.load(r.c, r.rows_c.at[t])
    load_m = [
        wire.load(r.m_joint, r.m_joint_v),
        wire.load(r.m_output, r.m_output_v),
        wire.load(r.m_expand, r.m_expand_v),
        wire.load(r.m_reduce, r.m_reduce_v),
        wire.load(r.first, r.first_v),
        wire.load(r.second, r.second_v),
    ]
    for copy in load_w:
        copy.wait()
    for k in range(4):
        for part in range(3):
            r.j_out[k, :, 128 * part : 128 * part + 128] = r.joint_v[
                :, 512 * part + 128 * k : 512 * part + 128 * k + 128
            ]
        r.w_out[k, :, 0:512] = r.output_v[...]
        r.w_out[k, :, 512:1024] = r.expand_v[:, 512 * k : 512 * k + 512]
        r.w_out[k, :, 1024:1536] = r.reduce_v[:, 512 * k : 512 * k + 512]
    load_v.wait()
    r.table[...] = jnp.zeros((128, 128), F32)
    column = lax.broadcasted_iota(jnp.int32, (128, 11), 0) - (16 * seq + 4 * t)
    own_vec = jnp.zeros((128, 11), F32)
    for j in range(4):
        own_vec = jnp.where(column == j, r.vectors_v[j : j + 1, :], own_vec)
    r.table[:, 0:11] = own_vec.astype(BF).astype(F32)
    r.v_own[...] = r.table[...].T[0:16, :]
    load_x.wait()
    load_c.wait()
    met()

    joint_t = trade_t(wire, place, r.j_out, r.j_in)
    for partner in place.row_t():
        joint_t.append(wire.push(r.v_own, r.v_in.at[t], partner))
    rest_t = trade_t(wire, place, r.w_out, r.w_in)
    x_rows = [wire.push(r.rows_x.at[t], r.rows_x.at[t], p) for p in place.row_t()]
    r.j_in[t] = r.j_out[t]
    r.v_in[t] = r.v_own[...]
    r.w_in[t] = r.w_out[t]
    arrive(joint_t)
    for k in range(4):
        r.j_rows[4 * k : 4 * k + 4, :] = r.j_in[k]
    keys, values = r.j_rows[:, 128:256], r.j_rows[:, 256:384]
    low16 = lax.broadcasted_iota(jnp.int32, (16, 128), 1) < 64
    own_block = r.wj.at[c, place.a, place.b]
    own_block[:, 0:128] = r.j_rows[:, 0:128].astype(BF)
    own_block[:, 128:256] = jnp.where(low16, keys, pltpu.roll(values, 64, 1)).astype(BF)
    own_block[:, 256:384] = jnp.where(low16, pltpu.roll(keys, 64, 1), values).astype(BF)
    own_block[:, 384:512] = ((r.v_in[0] + r.v_in[1]) + (r.v_in[2] + r.v_in[3])).astype(BF)
    joint_all = spread_plane(wire, place, r.wj)
    arrive(rest_t)
    for k in range(4):
        r.w_rows[4 * k : 4 * k + 4, :] = r.w_in[k]
    r.wr[c, z, x] = r.w_rows[...].astype(BF)
    block = r.wr.at[c, z, x]
    rest_b = [wire.push(block, block, partner) for partner in place.row_x()]

    half = ROT // 2
    lane = lax.rem(lax.broadcasted_iota(jnp.int32, (1, 128), 1), 64)
    frequency = jnp.zeros((1, 128), F32)
    for i in range(half):
        frequency = jnp.where(lax.rem(lane, half) == i, 10000.0 ** (-2.0 * i / ROT), frequency)
    frequency = jnp.where(lane < ROT, frequency, 0.0)

    def angles(i, _):
        index = 512 * seq + 128 * i + lax.broadcasted_iota(jnp.int32, (128, 1), 0)
        begin = jnp.zeros((128, 1), jnp.int32)
        finish = 0
        for j in range(4):
            finish = finish + r.lengths[0, j]
            begin = jnp.where(index >= finish, finish, begin)
        angle = (index - begin).astype(F32) * frequency
        r.cos[i] = jnp.cos(angle)
        r.sin[i] = jnp.sin(angle)
        return 0

    lax.fori_loop(0, 4, angles, 0)
    for copy in load_m:
        copy.wait()
    arrive(joint_all)
    joint_swap = swap_cores(wire, place, r.wj)
    arrive(rest_b)
    rest = Ring(wire, place, r.wr, z, lambda i: place.at(z=i))
    arrive(x_rows)
    c_rows = [wire.push(r.rows_c.at[t], r.rows_c.at[t], p) for p in place.row_t()]
    joint_swap.wait_recv()
    for k in range(4):
        own_vec = jnp.zeros((16, 128), F32)
        for i in range(4):
            for part in (r.wj[0, k, i, :, 384:512], r.wj[1, i, k, :, 384:512]):
                own_vec = own_vec + part.astype(F32)
        r.v[k] = own_vec
    natural(r.wj, r.w_joint, 0, 384)

    gain, shift = vec_row(r.v, 0), vec_row(r.v, 1)
    q_bias, k_bias, v_bias = r.v[t, 2:3, :], r.v[t, 3:4, :], r.v[t, 4:5, :]
    low_row = lax.broadcasted_iota(jnp.int32, (1, 128), 1) < 64
    pair_bias = (
        jnp.where(low_row, k_bias, pltpu.roll(v_bias, 64, 1)),
        jnp.where(low_row, pltpu.roll(k_bias, 64, 1), v_bias),
    )
    low = lax.broadcasted_iota(jnp.int32, (256, 128), 1) < 64

    def project(i, _):
        blocks, rows = pl.ds(2 * i, 2), pl.ds(256 * i, 256)
        normal, _rate = normalise(r.rows_x[blocks].reshape(256, 512))
        part = (normal * gain + shift).astype(BF)
        r.normed[blocks] = part.reshape(2, 128, 512)
        raw = dot(part, r.w_joint[...].reshape(512, 384))
        cosine, sine = r.cos[blocks].reshape(256, 128), r.sin[blocks].reshape(256, 128)
        query = turn(raw[:, 0:128] + q_bias, cosine, sine, 1.0)
        r.q_turned[i] = query.T.astype(BF)
        key_cos = jnp.where(low, cosine, 1.0)
        key_sin = jnp.where(low, sine, 0.0)
        for h in range(2):
            pair = raw[:, 128 + 128 * h : 256 + 128 * h] + pair_bias[h]
            r.kv_buf[h, rows, :] = turn(pair, key_cos, key_sin, 1.0).astype(BF)
        return 0

    lax.fori_loop(0, 2, project, 0)
    for i in range(2):
        for h in range(2):
            r.q_buf[h, :, 256 * i : 256 * i + 256] = r.q_turned[i, 64 * h : 64 * h + 64, :]
    kv_cross = []
    for i in range(2):
        rows = pl.ds(256 * i, 256)
        kv_cross.append(
            wire.push(r.kv_buf.at[1 - head, rows], r.kv.at[seq, rows], place.at(x=cross))
        )
    q_cross = wire.push(r.q_buf.at[1 - head], r.q_heads.at[1], place.at(x=cross, c=1 - c))
    kv_mate = wire.push(r.kv_buf.at[head], r.kv.at[seq], place.at(x=mate))
    kv_core = wire.push(r.kv_buf.at[head], r.kv.at[seq], sibling)
    r.kv[seq] = r.kv_buf[head]
    r.q_heads[0] = r.q_buf[head]
    attend_start(r, place)
    query_prepare(r, 0)
    r.sums[...] = jnp.zeros_like(r.sums)
    r.back_turned[...] = jnp.zeros_like(r.back_turned)
    for k in range(4):
        lanes = slice(128 * k, 128 * k + 128)
        keys = r.m_joint_v[:, 512 + 128 * k : 640 + 128 * k]
        values = r.m_joint_v[:, 1024 + 128 * k : 1152 + 128 * k]
        start = 384 * k
        r.m_own[0, :, start : start + 128] = r.m_joint_v[:, lanes]
        r.m_own[0, :, start + 128 : start + 256] = jnp.concatenate(
            [keys[:, 0:64], values[:, 0:64]], axis=1
        )
        r.m_own[0, :, start + 256 : start + 384] = jnp.concatenate(
            [keys[:, 64:128], values[:, 64:128]], axis=1
        )
    r.m_own[0, :, 1536:2048] = jnp.zeros((4, 512), F32)
    r.m_own[1, :, 0:512] = r.m_output_v[...]
    r.m_own[1, :, 512:2048] = jnp.zeros((4, 1536), F32)
    r.m_own[2] = r.m_expand_v[...]
    r.m_own[3] = r.m_reduce_v[...]
    rest.hand_on()
    kv_core.wait_recv()
    keys_prepare(r, x)
    score_column(r, place, x, 0, diagonal=True)
    at_cross, at_mate = 2 * cross + c, 2 * mate + c
    at_far = 2 * (3 - mate) + c
    kv_far, kv_sent, far_sent = [], [], []
    for i in range(2):
        kv_cross[i].wait_recv()
        part = r.kv.at[at_cross, pl.ds(256 * i, 256)]
        kv_far.append(wire.push(part, part, place.at(x=mate)))
        kv_sent.append(wire.push(part, part, sibling))
    kv_mate.wait_recv()
    mate_sent = wire.push(r.kv.at[at_mate], r.kv.at[at_mate], sibling)
    rest.close()
    q_cross.wait_recv()
    query_prepare(r, 1)
    score_column(r, place, x, 1)
    mate_sent.wait_recv()
    keys_prepare(r, mate)
    score_column(r, place, mate, 0)
    score_column(r, place, mate, 1)
    arrive([*c_rows, *rest.swaps])
    by_row(r.wr, r.w_output, 0, 512)
    by_row(r.wr, r.w_expand, 512, 1024)
    by_row(r.wr, r.w_reduce, 1024, 1536)
    out_rows = r.w_output[pl.ds(8 * t, 8)].reshape(128, 512)
    grad = dot_cols(out_rows, r.rows_c[...].reshape(512, 512)).astype(BF)
    r.g_buf[0] = grad[0:64, :]
    r.g_buf[1] = grad[64:128, :]
    g_cross = wire.push(r.g_buf.at[1 - head], r.g_heads.at[1], place.at(x=cross, c=1 - c))
    r.g_heads[0] = r.g_buf[head]
    grad_prepare(r, 0)
    early = trade_t(wire, place, r.m_own, r.m_early)

    bias = jnp.concatenate([r.v[k, pl.ds(7 + t, 1), :] for k in range(4)], axis=1)

    def feed_forward(i, sums):
        blocks = pl.ds(2 * i, 2)
        part = r.normed[blocks].reshape(256, 512)
        wide = dot(part, r.w_expand[...].reshape(512, 512)) + bias
        square = wide * wide
        curve = jnp.tanh(0.7978845608 * (wide + 0.044715 * (square * wide)))
        r.hidden[blocks] = (0.5 * wide * (1.0 + curve)).astype(BF).reshape(2, 128, 512)
        slope = 0.5 * (1.0 + curve) + (0.5 * 0.7978845608) * wide * (1.0 - curve * curve) * (
            1.0 + (3 * 0.044715) * square
        )
        part = r.rows_c[blocks].reshape(256, 512)
        back = dot(part, r.w_reduce[...].reshape(512, 512))
        grad = (back * slope).astype(BF)
        r.pre[blocks] = grad.reshape(2, 128, 512)
        return sums + jnp.sum(grad.astype(F32), axis=0, keepdims=True)

    hidden_sum = lax.fori_loop(0, 2, feed_forward, jnp.zeros((1, 512), F32))
    for i in range(2):
        kv_far[i].wait_recv()
        part = r.kv.at[at_far, pl.ds(256 * i, 256)]
        far_sent.append(wire.push(part, part, sibling))
    for j in range(4):
        lanes = slice(128 * j, 128 * j + 128)
        expand_grad = dot_rows(
            r.normed[:, :, lanes].reshape(512, 128), r.pre[...].reshape(512, 512)
        )
        by_core(r.gf, j, expand_grad.astype(BF), 0, 512)
        reduce_grad = dot_rows(
            r.rows_c[:, :, lanes].reshape(512, 128), r.hidden[...].reshape(512, 512)
        )
        by_core(r.gf, j, reduce_grad.astype(BF), 512, 1024)
    gf_swap = sum_cores(wire, place, r.gf, r.gf_core)
    far = 3 - mate
    arrive(kv_sent)
    keys_prepare(r, cross)
    score_column(r, place, cross, 0)
    score_column(r, place, cross, 1, diagonal=True)
    arrive(far_sent)
    keys_prepare(r, far)
    score_column(r, place, far, 0)
    score_column(r, place, far, 1)
    gf_swap.wait_recv()
    for a in range(4):
        r.gf_chip[a] = (r.gf[c, a].astype(F32) + r.gf_core[a].astype(F32)).astype(BF)
    gf_z = []
    for k in range(1, 4):
        goal = ring(z, k)
        gf_z.append(wire.push(r.gf_chip.at[goal], r.gf_z.at[k - 1], place.at(z=goal)))
    weigh_values(r, place, 1)
    out_cross = wire.push(r.out_low.at[1], r.out_heads.at[head], place.at(x=cross, c=1 - c))
    weigh_values(r, place, 0)
    r.out_heads[head] = r.out_low[0]
    g_cross.wait_recv()
    grad_prepare(r, 1)
    for slot in range(2):
        r.centre[slot] = jnp.sum(
            r.out_turned[slot] * r.g_heads[slot].astype(F32), axis=0, keepdims=True
        )

    dk_swap = []

    def chip_sum(index):
        return r.dk[c, index].astype(F32) + r.dk_in[index].astype(F32)

    dk_sent = []

    def send_column(step, column):
        dk_swap[step].wait_recv()
        r.dk_chip[step] = chip_sum(column).astype(BF)
        dk_sent.append(
            wire.push(r.dk_chip.at[step], r.dk_got.at[step], place.at(x=column))
        )

    backward_cross(r, place)
    back_cross = wire.push(r.back_low.at[1], r.back_heads.at[head], place.at(x=cross, c=1 - c))
    out_cross.wait_recv()
    turned = r.out_heads[...].reshape(128, 512)
    r.pair_out[...] = turned
    out_grad = dot(turned, r.rows_c[...].reshape(512, 512)).astype(BF)
    for j in range(4):
        r.out_cols[j] = out_grad[:, 128 * j : 128 * j + 128]
    out_cols = trade_t(wire, place, r.out_cols, r.out_in)
    r.out_in[t] = r.out_cols[t]
    columns = (far, cross, mate, x)
    for step, column in enumerate(columns):
        backward_column(r, place, column, diagonal=step == 3)
        dk_swap.append(wire.push(r.dk.at[1 - c, column], r.dk_in.at[column], sibling))
        if step > 0:
            send_column(step - 1, columns[step - 1])
    r.back_low[0] = (r.back_turned[...] * (HD ** -0.5)).astype(BF)
    r.back_heads[head] = r.back_low[0]
    arrive(gf_z)
    r.gf_line[...] = total(r.gf_chip[z], r.gf_z).astype(BF)
    gf_x = []
    for k in range(1, 4):
        goal = ring(x, k)
        gf_x.append(wire.push(r.gf_line.at[goal], r.gf_x.at[k - 1], place.at(x=goal)))
    arrive(out_cols)
    for j in range(4):
        by_owner(r.go, j, r.out_in[j], 0, 128)
    go_swap = sum_cores(wire, place, r.go, r.go_core)

    def feed_out(i, _):
        blocks = pl.ds(2 * i, 2)
        part = r.hidden[blocks].reshape(256, 512)
        r.feed[blocks] = dot_cols(part, r.w_reduce[...].reshape(512, 512)).reshape(2, 128, 512)
        part = r.pre[blocks].reshape(256, 512)
        r.row_grad[blocks] = dot_cols(part, r.w_expand[...].reshape(512, 512)).reshape(2, 128, 512)
        return 0

    lax.fori_loop(0, 2, feed_out, 0)
    go_swap.wait_recv()
    for a in range(4):
        r.go_chip[a] = (r.go[c, a].astype(F32) + r.go_core[a].astype(F32)).astype(BF)
    go_all = scatter_plane(wire, place, r.go_chip, r.go_in)
    out_rows = r.w_output[pl.ds(8 * t, 8)].reshape(128, 512)
    for i in range(2):
        blocks, lanes = slice(2 * i, 2 * i + 2), slice(256 * i, 256 * i + 256)
        part = r.feed[blocks].reshape(256, 512) + dot_rows(r.pair_out[:, lanes], out_rows)
        r.out_part[blocks] = part.astype(BF).reshape(2, 128, 512)
    out_parts = trade_t(wire, place, r.out_part, r.out_got)
    r.out_got[t] = r.out_part[t]
    back_cross.wait_recv()
    back = r.back_heads[...].reshape(128, 512).astype(F32).T
    cosine, sine = r.cos[...].reshape(512, 128), r.sin[...].reshape(512, 128)
    r.joint_out[:, 0:128] = turn(back, cosine, sine, -1.0).astype(BF)
    low = lax.broadcasted_iota(jnp.int32, (128, 128), 1) < 64
    arrive([dk_swap[3], *dk_sent])
    r.dkv[head] = (chip_sum(x) + r.dk_got[2].astype(F32)).astype(BF)
    r.dkv[1 - head] = (r.dk_got[0].astype(F32) + r.dk_got[1].astype(F32)).astype(BF)
    for h in range(2):
        for i in range(4):
            rows = pl.ds(128 * i, 128)
            key_cos = jnp.where(low, r.cos[i], 1.0)
            key_sin = jnp.where(low, r.sin[i], 0.0)
            r.joint_out[rows, 128 + 128 * h : 256 + 128 * h] = turn(
                r.dkv[h, rows, :].astype(F32), key_cos, key_sin, -1.0
            ).astype(BF)
    for j in range(4):
        part = r.normed[:, :, 128 * j : 128 * j + 128].reshape(512, 128)
        by_owner(r.gj, j, dot_rows(part, r.joint_out[...]).astype(BF), 0, 384)
    gj_swap = sum_cores(wire, place, r.gj, r.gj_core)

    r.vp[0] = jnp.zeros((4, 16, 128), F32)
    shift_sum = jnp.zeros((1, 512), F32)
    gain_sum = jnp.zeros((1, 512), F32)
    for i in range(4):
        rows = pl.ds(128 * i, 128)
        part = r.row_grad[i] + dot_cols(r.joint_out[rows, :], r.w_joint[...].reshape(512, 384))
        r.back_part[i] = part.astype(BF)
        normal, _rate = normalise(r.rows_x[i])
        shift_sum = shift_sum + jnp.sum(part, axis=0, keepdims=True)
        gain_sum = gain_sum + jnp.sum(part * normal, axis=0, keepdims=True)
    gj_swap.wait_recv()
    for a in range(4):
        r.gj_chip[a] = (r.gj[c, a].astype(F32) + r.gj_core[a].astype(F32)).astype(BF)
    gj_all = scatter_plane(wire, place, r.gj_chip, r.gj_in)
    back_parts = trade_t(wire, place, r.back_part, r.back_got)
    r.back_got[t] = r.back_part[t]
    out_sum = jnp.sum(r.rows_c[t].astype(F32), axis=0, keepdims=True)
    joint_sum = jnp.sum(r.joint_out[...].astype(F32), axis=0, keepdims=True)
    one, two = joint_sum[:, 128:256], joint_sum[:, 256:384]
    for k in range(4):
        lanes = slice(128 * k, 128 * k + 128)
        r.vp[0, k, 0:1, :] = gain_sum[:, lanes]
        r.vp[0, k, 1:2, :] = shift_sum[:, lanes]
        r.vp[0, k, 5:6, :] = out_sum[:, lanes]
        r.vp[0, k, 6:7, :] = out_sum[:, lanes]
        r.vp[0, k, pl.ds(7 + t, 1), :] = hidden_sum[:, lanes]
    r.vp[0, t, 2:3, :] = joint_sum[:, 0:128]
    r.vp[0, t, 3:4, :] = jnp.where(low_row, one, pltpu.roll(two, 64, 1))
    r.vp[0, t, 4:5, :] = jnp.where(low_row, pltpu.roll(one, 64, 1), two)
    vp_swap = wire.push(r.vp.at[0], r.vp_core, sibling)
    arrive(gf_x)
    gf_own = total(r.gf_line[x], r.gf_x)
    arrive(go_all)
    go_own = add_plane(r.go_chip[place.a, place.b], r.go_in)
    for k in range(4):
        r.early_out[k, :, 0:1024] = gf_own[4 * k : 4 * k + 4, :]
        r.early_out[k, :, 1024:1152] = go_own[4 * k : 4 * k + 4, :]
    r.gm_out[1, :, 0:128] = go_own.astype(BF)
    r.gm_out[2] = gf_own[:, 0:512].astype(BF)
    r.gm_out[3] = gf_own[:, 512:1024].astype(BF)
    gm_first = wire.block(4)
    gm_widths = (384, 128, 512, 512)

    def to_newton(w, sender):
        lanes = slice(0, gm_widths[w])
        return wire.offer(
            gm_first, r.gm_out.at[w, :, lanes], r.gm_in.at[sender, :, lanes], sender, w,
            place.at(t=w),
        )

    def send_newton(w):
        @pl.when(t != w)
        def _():
            to_newton(w, t).start()

        @pl.when(t == w)
        def _():
            r.gm_in[w, :, 0 : gm_widths[w]] = r.gm_out[w, :, 0 : gm_widths[w]]

    for w in (1, 2, 3):
        send_newton(w)
    early_t = trade_t(wire, place, r.early_out, r.early_in)
    r.early_in[t] = r.early_out[t]

    arrive(early)
    r.m_early[t] = r.m_own[t]
    for k in range(4):
        r.m_old[4 * k : 4 * k + 4, :] = r.m_early[k]
    vp_swap.wait_recv()
    r.vp[1] = r.vp[0] + r.vp_core[...]
    vp_z = [wire.push(r.vp.at[1], r.vp_z.at[k], p) for k, p in enumerate(place.row_z())]

    arrive(gj_all)
    gj_own = add_plane(r.gj_chip[place.a, place.b], r.gj_in)
    r.gm_out[0, :, 0:384] = gj_own.astype(BF)
    send_newton(0)
    for k in range(4):
        r.late_out[k] = gj_own[4 * k : 4 * k + 4, :]
    late_t = trade_t(wire, place, r.late_out, r.late_in)
    r.late_in[t] = r.late_out[t]
    arrive(vp_z)
    r.vp[2] = total(r.vp[1], r.vp_z)
    vp_x = [wire.push(r.vp.at[2], r.vp_x.at[k], p) for k, p in enumerate(place.row_x())]

    for w in range(4):

        @pl.when(t == w)
        def _(w=w):
            width = gm_widths[w]
            for sender in range(4):
                if sender != w:
                    to_newton(w, sender).wait_recv()
            for k in range(4):
                lanes = slice(width * k, width * k + width)
                value = muon_beta * r.m_old[:, lanes] + r.gm_in[k, :, 0:width].astype(F32)
                if width * k < 1536:
                    r.momentum[c, place.a, place.b, :, lanes] = value.astype(BF)
                else:
                    r.extra[c, place.a, place.b] = value.astype(BF)
            if w == 1:
                r.momentum[c, place.a, place.b, :, 512:1536] = jnp.zeros((16, 1024), BF)

    m_b = spread_b(wire, place, r.momentum)

    extra_first = wire.block(16)

    def extra_copies():
        block = r.extra.at[c, place.a, place.b]
        copies = []
        for k, (a, b) in enumerate(place.plane()):
            copies.append(
                wire.offer(extra_first, block, block, k, k, place.at_ab(a, b))
            )
        return copies

    def extra_swap():
        block = r.extra.at[c]
        return wire.offer(extra_first, block, block, 15, 15, sibling)

    @pl.when(t >= 2)
    def _():
        for copy in extra_copies():
            copy.start()

    arrive(early_t)
    for k in range(4):
        part = r.early_in[k]
        r.g_expand[:, 512 * k : 512 * k + 512] = part[:, 0:512]
        r.g_reduce[:, 512 * k : 512 * k + 512] = part[:, 512:1024]
        r.g_output[:, 128 * k : 128 * k + 128] = part[:, 1024:1152]
    arrive(late_t)
    for k in range(4):
        unpair(r.g_joint, r.late_in[k], k)
    for old, grad, new in (
        (r.m_joint_v, r.g_joint, r.n_joint),
        (r.m_output_v, r.g_output, r.n_output),
        (r.m_expand_v, r.g_expand, r.n_expand),
        (r.m_reduce_v, r.g_reduce, r.n_reduce),
    ):
        new[...] = muon_beta * old[...] + grad[...]
    arrive(vp_x)
    r.vp[3] = total(r.vp[2], r.vp_x)
    vp_t = [wire.push(r.vp.at[3], r.vp_t.at[k], p) for k, p in enumerate(place.row_t())]
    arrive(out_parts)
    arrive(back_parts)
    arrive(m_b)
    whole = Ring(wire, place, r.momentum, place.a, place.at_a)
    whole.hand_on()
    wide = r.rows_x[t].astype(F32)
    feed = r.out_got[0].astype(F32)
    back = r.back_got[0].astype(F32)
    for k in range(1, 4):
        feed = feed + r.out_got[k].astype(F32)
        back = back + r.back_got[k].astype(F32)
    r.block_output[...] = (wide + feed + vec_row(r.v, 5) + vec_row(r.v, 6)).astype(BF)
    normal, rate = normalise(r.rows_x[t])
    scaled = back * gain
    mean_one = jnp.mean(scaled, axis=-1, keepdims=True)
    mean_two = jnp.mean(scaled * normal, axis=-1, keepdims=True)
    r.input_grad[...] = r.rows_c[t].astype(F32) + rate * (scaled - mean_one - normal * mean_two)
    whole.close()
    arrive(vp_t)
    r.vec_sum[...] = total(r.vp[3], r.vp_t)
    r.table[0:16, :] = r.vec_sum[z]
    r.table[...] = r.table[...].T
    vector_grad = r.table[pl.ds(pl.multiple_of(16 * seq + 4 * t, 4), 4), 0:11]
    r.vector_grad[...] = vector_grad
    first_next = beta_first * r.first_v[...] + (1.0 - beta_first) * vector_grad
    second_next = (
        beta_second * r.second_v[...] + (1.0 - beta_second) * vector_grad * vector_grad
    )
    r.second_next[...] = second_next
    first_hat = first_next / (1.0 - beta_first**STEP)
    second_hat = second_next / (1.0 - beta_second**STEP)
    r.vector_next[...] = r.vectors_v[...] - vector_rate * first_hat / (
        jnp.sqrt(second_hat) + adam_epsilon
    )
    @pl.when(t >= 2)
    def _():
        for copy in extra_copies():
            copy.wait_recv()
        extra_swap().start()
        extra_swap().wait_recv()

    arrive(whole.swaps)

    high, small = newton(r, place)
    both = jnp.concatenate([high, small], axis=0)
    for k in range(3):
        lanes = slice(512 * k, 512 * k + 512)
        rows = dot(both, r.momentum[:, :, :, :, lanes].reshape(512, 512))
        r.m_rows[:, lanes] = rows[0:16] + rows[16:32]

    @pl.when(t >= 2)
    def _():
        rows = dot(both, r.extra[...].reshape(512, 512))
        r.m_rows[:, 1536:2048] = rows[0:16] + rows[16:32]

    @pl.when(t < 2)
    def _():
        r.m_rows[:, 1536:2048] = jnp.zeros((16, 512), F32)

    for k in range(4):
        for p in range(4):
            r.u_rows[k, 4 * p : 4 * p + 4, :] = r.m_rows[
                4 * k : 4 * k + 4, 512 * p : 512 * p + 512
            ]
    r.u_out[...] = r.u_rows[...].astype(BF)
    u_t = trade_t(wire, place, r.u_out, r.u_in)
    r.u_in[t] = r.u_out[t]
    wire.drain()
    for w in range(4):

        @pl.when(t != w)
        def _(w=w):
            to_newton(w, t).wait_send()

    @pl.when(t >= 2)
    def _():
        for copy in extra_copies():
            copy.wait_send()
        extra_swap().wait_send()

    arrive(u_t)
    r.u_rows[...] = r.u_in[...].astype(F32)
    for k in range(4):
        for p in range(4):
            r.u_wide[k, :, 512 * p : 512 * p + 512] = r.u_rows[k, 4 * p : 4 * p + 4, :]
    for k in range(4):
        unpair(r.u_joint, r.u_wide[0, :, 384 * k : 384 * k + 384], k)
    for k, (old, change, new) in enumerate(
        (
            (r.joint_v, r.u_joint, r.u_joint),
            (r.output_v, r.u_wide.at[1, :, pl.ds(0, 512)], r.u_output),
            (r.expand_v, r.u_wide.at[2], r.u_expand),
            (r.reduce_v, r.u_wide.at[3], r.u_reduce),
        )
    ):
        factor = muon_rate * 0.2 * math.sqrt(max(D, WIDTHS[k]))
        new[...] = old[...] * (1.0 - muon_rate * muon_decay) - factor * change[...]
    wire.drain()


def block_stage(*arrays):
    return pl.pallas_call(
        block_kernel,
        out_shape=tuple(shape(dims, dtype) for _, dims, dtype in OUTPUTS),
        in_specs=[SMEM] + [ANY] * (len(INPUTS) - 1),
        out_specs=(VMEM,) * len(OUTPUTS),
        scratch_shapes=[pltpu.VMEM(dims, dtype) for _, dims, dtype in SCRATCH]
        + [
            pltpu.SemaphoreType.DMA((PUSHES,)),
            pltpu.SemaphoreType.DMA((PUSHES,)),
            pltpu.SemaphoreType.DMA((LOADS,)),
        ],
        compiler_params=pltpu.CompilerParams(
            collective_id=1, has_side_effects=True, vmem_limit_bytes=56 << 20
        ),
        name="block",
    )(*arrays)


def write_kernel(*refs):
    count = len(OUTPUTS)
    sem = refs[-1]
    copies = []
    for k in range(count):
        copy = pltpu.make_async_copy(refs[k], refs[count + k], sem.at[k])
        copy.start()
        copies.append(copy)
    for copy in copies:
        copy.wait()


def write_stage(*arrays):
    count = len(arrays)
    return pl.pallas_call(
        write_kernel,
        out_shape=tuple(shape(a.shape, a.dtype) for a in arrays),
        in_specs=[VMEM] * count,
        out_specs=(ANY,) * count,
        scratch_shapes=[pltpu.SemaphoreType.DMA((count,))],
        name="write",
    )(*arrays)


def shards(
    block_input,
    cotangent,
    doc_lengths,
    joint_weight,
    output_weight,
    expand_weight,
    reduce_weight,
    joint_moment,
    output_moment,
    expand_moment,
    reduce_moment,
    vectors,
    first_moment,
    second_moment,
):
    results = block_stage(
        doc_lengths, block_input, cotangent, joint_weight, output_weight, expand_weight,
        reduce_weight, vectors.T, joint_moment, output_moment, expand_moment, reduce_moment,
        first_moment.T, second_moment.T,
    )
    results = write_stage(*results)
    return (*results[12:14], *results[0:12], *[part.T for part in results[14:]])


def solution(mesh):
    rows = P(("fsdp", "seq", "tensor"), None)
    columns = P(None, ("fsdp", "seq", "tensor"))
    return jax.shard_map(
        shards,
        mesh=mesh,
        in_specs=(rows, rows, P("fsdp", None)) + (rows,) * 8 + (columns,) * 3,
        out_specs=(rows,) * 14 + (columns,) * 3,
        check_vma=False,
    )
```

profile of v0, /device:TPU:1, one launch (start us, length us, event | category | flops | bytes accessed | tf_op | source)
XLA Modules:
  0.0 102.0 jit_solution(9115599901533466814)
XLA Ops:
  0.7 98.9 %block.1 = (f32[4,1536]{1,0:T(4,128)}, f32[4,512]{1,0:T(4,128)}, f32[4,2048]{1,0:T(4,128)}, f32[4,2048]{1,0:T(4,128)}, f32[4,1536]{1,0:T(4,128)}, /*index=5*/f32...) custom-call(s32[1,4]{1,0:T(1,128)} %refs_0_.1, ...), custom_call_target="tpu_custom_call" | custom-call | tf_op jit(solution)/shard_map/block/pallas_call | solution.py:1341
  99.6 2.2 %write.1 = (f32[4,1536]{1,0:T(4,128)}, f32[4,512]{1,0:T(4,128)}, f32[4,2048]{1,0:T(4,128)}, f32[4,2048]{1,0:T(4,128)}, f32[4,1536]{1,0:T(4,128)}, /*index=5*/f32...) custom-call(f32[4,1536]{1,0:T(4,128)} %get-tuple-element.51.refs_0_,, ...), custom_call_target="tpu_custom_call" | custom-call | tf_op jit(solution)/shard_map/write/pallas_call | solution.py:1373
where the time goes:
time: 102 us
  Pallas kernels  101 us (99%)
    pallas_call x1, Pallas kernels, block_stage(): pl.pallas_call(block_kernel, out_shape=tuple((shape(dims, dtype) for _, d...  98.9 us
    pallas_call x1, Pallas kernels, write_stage(): pl.pallas_call(write_kernel, out_shape=tuple((shape(a.shape, a.dtype) for...  2.22 us

commit v1 on v0

--- a/solution.py
+++ b/solution.py
@@ -648,19 +648,12 @@
         return row == lax.broadcasted_iota(jnp.int32, (size, 512), 1)
 
     def fill(i, trace):
-        value = jnp.zeros((size, 512), F32)
+        value = r.gram[...]
         for k in range(3):
             lanes = slice(512 * k, 512 * k + 512)
             right = r.momentum[:, :, :, :, lanes].reshape(512, 512)
             value = value + dot_cols(right, right)
-        r.gram[rows(i), :] = value
-
-        @pl.when(place.t >= 2)
-        def _():
-            right = r.extra[...].reshape(512, 512)
-            r.gram[rows(i), :] += dot_cols(right, right)
-
-        value = r.gram[rows(i), :]
+        r.gram[...] = value
         return trace + jnp.sum(jnp.where(diagonal(i), value, 0.0), keepdims=True)
 
     trace = lax.fori_loop(0, blocks, fill, jnp.zeros((1, 1), F32))
@@ -768,16 +761,12 @@
         wire.load(r.first, r.first_v),
         wire.load(r.second, r.second_v),
     ]
-    for copy in load_w:
-        copy.wait()
+    load_w[0].wait()
     for k in range(4):
         for part in range(3):
             r.j_out[k, :, 128 * part : 128 * part + 128] = r.joint_v[
                 :, 512 * part + 128 * k : 512 * part + 128 * k + 128
             ]
-        r.w_out[k, :, 0:512] = r.output_v[...]
-        r.w_out[k, :, 512:1024] = r.expand_v[:, 512 * k : 512 * k + 512]
-        r.w_out[k, :, 1024:1536] = r.reduce_v[:, 512 * k : 512 * k + 512]
     load_v.wait()
     r.table[...] = jnp.zeros((128, 128), F32)
     column = lax.broadcasted_iota(jnp.int32, (128, 11), 0) - (16 * seq + 4 * t)
@@ -786,14 +775,20 @@
         own_vec = jnp.where(column == j, r.vectors_v[j : j + 1, :], own_vec)
     r.table[:, 0:11] = own_vec.astype(BF).astype(F32)
     r.v_own[...] = r.table[...].T[0:16, :]
-    load_x.wait()
-    load_c.wait()
     met()
 
     joint_t = trade_t(wire, place, r.j_out, r.j_in)
     for partner in place.row_t():
         joint_t.append(wire.push(r.v_own, r.v_in.at[t], partner))
+    for copy in load_w[1:]:
+        copy.wait()
+    for k in range(4):
+        r.w_out[k, :, 0:512] = r.output_v[...]
+        r.w_out[k, :, 512:1024] = r.expand_v[:, 512 * k : 512 * k + 512]
+        r.w_out[k, :, 1024:1536] = r.reduce_v[:, 512 * k : 512 * k + 512]
     rest_t = trade_t(wire, place, r.w_out, r.w_in)
+    load_x.wait()
+    load_c.wait()
     x_rows = [wire.push(r.rows_x.at[t], r.rows_x.at[t], p) for p in place.row_t()]
     r.j_in[t] = r.j_out[t]
     r.v_in[t] = r.v_own[...]
@@ -841,9 +836,9 @@
     arrive(joint_all)
     joint_swap = swap_cores(wire, place, r.wj)
     arrive(rest_b)
+    c_rows = [wire.push(r.rows_c.at[t], r.rows_c.at[t], p) for p in place.row_t()]
     rest = Ring(wire, place, r.wr, z, lambda i: place.at(z=i))
     arrive(x_rows)
-    c_rows = [wire.push(r.rows_c.at[t], r.rows_c.at[t], p) for p in place.row_t()]
     joint_swap.wait_recv()
     for k in range(4):
         own_vec = jnp.zeros((16, 128), F32)
@@ -1198,24 +1193,39 @@
 
     m_b = spread_b(wire, place, r.momentum)
 
-    extra_first = wire.block(16)
-
-    def extra_copies():
+    extra_first = wire.block(7)
+
+    def extra_line():
         block = r.extra.at[c, place.a, place.b]
-        copies = []
-        for k, (a, b) in enumerate(place.plane()):
-            copies.append(
-                wire.offer(extra_first, block, block, k, k, place.at_ab(a, b))
-            )
-        return copies
+        return [
+            wire.offer(extra_first, block, block, k, k, place.at_b(ring(place.b, k)))
+            for k in range(1, 4)
+        ]
+
+    def extra_lines():
+        block = r.extra.at[c, place.a]
+        return [
+            wire.offer(extra_first, block, block, 3 + k, 3 + k, place.at_a(ring(place.a, k)))
+            for k in range(1, 4)
+        ]
 
     def extra_swap():
         block = r.extra.at[c]
-        return wire.offer(extra_first, block, block, 15, 15, sibling)
+        return wire.offer(extra_first, block, block, 0, 0, sibling)
 
     @pl.when(t >= 2)
     def _():
-        for copy in extra_copies():
+        for copy in extra_line():
+            copy.start()
+
+    arrive(m_b)
+    whole = Ring(wire, place, r.momentum, place.a, place.at_a)
+
+    @pl.when(t >= 2)
+    def _():
+        for copy in extra_line():
+            copy.wait_recv()
+        for copy in extra_lines():
             copy.start()
 
     arrive(early_t)
@@ -1239,9 +1249,6 @@
     vp_t = [wire.push(r.vp.at[3], r.vp_t.at[k], p) for k, p in enumerate(place.row_t())]
     arrive(out_parts)
     arrive(back_parts)
-    arrive(m_b)
-    whole = Ring(wire, place, r.momentum, place.a, place.at_a)
-    whole.hand_on()
     wide = r.rows_x[t].astype(F32)
     feed = r.out_got[0].astype(F32)
     back = r.back_got[0].astype(F32)
@@ -1254,6 +1261,14 @@
     mean_one = jnp.mean(scaled, axis=-1, keepdims=True)
     mean_two = jnp.mean(scaled * normal, axis=-1, keepdims=True)
     r.input_grad[...] = r.rows_c[t].astype(F32) + rate * (scaled - mean_one - normal * mean_two)
+    whole.hand_on()
+
+    @pl.when(t >= 2)
+    def _():
+        for copy in extra_lines():
+            copy.wait_recv()
+        extra_swap().start()
+
     whole.close()
     arrive(vp_t)
     r.vec_sum[...] = total(r.vp[3], r.vp_t)
@@ -1273,10 +1288,13 @@
     )
     @pl.when(t >= 2)
     def _():
-        for copy in extra_copies():
-            copy.wait_recv()
-        extra_swap().start()
         extra_swap().wait_recv()
+        columns = r.extra[...].reshape(512, 512)
+        r.gram[...] = dot_cols(columns, columns)
+
+    @pl.when(t < 2)
+    def _():
+        r.gram[...] = jnp.zeros((512, 512), F32)
 
     arrive(whole.swaps)
 
@@ -1313,7 +1331,7 @@
 
     @pl.when(t >= 2)
     def _():
-        for copy in extra_copies():
+        for copy in extra_line() + extra_lines():
             copy.wait_send()
         extra_swap().wait_send()
 

time: 102 us -> 101 us (level)
  no operation moved by 1% of the time
where the time goes in v1:
time: 101 us
  Pallas kernels  100 us (99%)
    pallas_call x1, Pallas kernels, block_stage(): pl.pallas_call(block_kernel, out_shape=tuple((shape(dims, dtype) for _, d...  98 us
    pallas_call x1, Pallas kernels, write_stage(): pl.pallas_call(write_kernel, out_shape=tuple((shape(a.shape, a.dtype) for...  2.22 us

profile of v1, /device:TPU:1, one launch (start us, length us, event | category | flops | bytes accessed | tf_op | source)
XLA Modules:
  0.0 101.0 jit_solution(16265289140578094625)
XLA Ops:
  0.7 98.0 %block.1 = (f32[4,1536]{1,0:T(4,128)}, f32[4,512]{1,0:T(4,128)}, f32[4,2048]{1,0:T(4,128)}, f32[4,2048]{1,0:T(4,128)}, f32[4,1536]{1,0:T(4,128)}, /*index=5*/f32...) custom-call(s32[1,4]{1,0:T(1,128)} %refs_0_.1, ...), custom_call_target="tpu_custom_call" | custom-call | tf_op jit(solution)/shard_map/block/pallas_call | solution.py:1359
  98.6 2.2 %write.1 = (f32[4,1536]{1,0:T(4,128)}, f32[4,512]{1,0:T(4,128)}, f32[4,2048]{1,0:T(4,128)}, f32[4,2048]{1,0:T(4,128)}, f32[4,1536]{1,0:T(4,128)}, /*index=5*/f32...) custom-call(f32[4,1536]{1,0:T(4,128)} %get-tuple-element.51.refs_0_,, ...), custom_call_target="tpu_custom_call" | custom-call | tf_op jit(solution)/shard_map/write/pallas_call | solution.py:1391

commit v2 on v1

--- a/solution.py
+++ b/solution.py
@@ -877,13 +877,13 @@
     for i in range(2):
         for h in range(2):
             r.q_buf[h, :, 256 * i : 256 * i + 256] = r.q_turned[i, 64 * h : 64 * h + 64, :]
+    q_cross = wire.push(r.q_buf.at[1 - head], r.q_heads.at[1], place.at(x=cross, c=1 - c))
     kv_cross = []
     for i in range(2):
         rows = pl.ds(256 * i, 256)
         kv_cross.append(
             wire.push(r.kv_buf.at[1 - head, rows], r.kv.at[seq, rows], place.at(x=cross))
         )
-    q_cross = wire.push(r.q_buf.at[1 - head], r.q_heads.at[1], place.at(x=cross, c=1 - c))
     kv_mate = wire.push(r.kv_buf.at[head], r.kv.at[seq], place.at(x=mate))
     kv_core = wire.push(r.kv_buf.at[head], r.kv.at[seq], sibling)
     r.kv[seq] = r.kv_buf[head]

time: 101 us -> 101 us (level)
  no operation moved by 1% of the time
where the time goes in v2:
time: 101 us
  Pallas kernels  100 us (99%)
    pallas_call x1, Pallas kernels, block_stage(): pl.pallas_call(block_kernel, out_shape=tuple((shape(dims, dtype) for _, d...  97.9 us
    pallas_call x1, Pallas kernels, write_stage(): pl.pallas_call(write_kernel, out_shape=tuple((shape(a.shape, a.dtype) for...  2.22 us

profile of v2, /device:TPU:1, one launch (start us, length us, event | category | flops | bytes accessed | tf_op | source)
XLA Modules:
  0.0 101.0 jit_solution(2954052703988534606)
XLA Ops:
  0.7 97.9 %block.1 = (f32[4,1536]{1,0:T(4,128)}, f32[4,512]{1,0:T(4,128)}, f32[4,2048]{1,0:T(4,128)}, f32[4,2048]{1,0:T(4,128)}, f32[4,1536]{1,0:T(4,128)}, /*index=5*/f32...) custom-call(s32[1,4]{1,0:T(1,128)} %refs_0_.1, ...), custom_call_target="tpu_custom_call" | custom-call | tf_op jit(solution)/shard_map/block/pallas_call | solution.py:1359
  98.6 2.2 %write.1 = (f32[4,1536]{1,0:T(4,128)}, f32[4,512]{1,0:T(4,128)}, f32[4,2048]{1,0:T(4,128)}, f32[4,2048]{1,0:T(4,128)}, f32[4,1536]{1,0:T(4,128)}, /*index=5*/f32...) custom-call(f32[4,1536]{1,0:T(4,128)} %get-tuple-element.51.refs_0_,, ...), custom_call_target="tpu_custom_call" | custom-call | tf_op jit(solution)/shard_map/write/pallas_call | solution.py:1391

commit v3 on v2

--- a/solution.py
+++ b/solution.py
@@ -1021,6 +1021,14 @@
 
     backward_cross(r, place)
     back_cross = wire.push(r.back_low.at[1], r.back_heads.at[head], place.at(x=cross, c=1 - c))
+    columns = (far, cross, mate, x)
+    for step, column in enumerate(columns):
+        backward_column(r, place, column, diagonal=step == 3)
+        dk_swap.append(wire.push(r.dk.at[1 - c, column], r.dk_in.at[column], sibling))
+        if step > 0:
+            send_column(step - 1, columns[step - 1])
+    r.back_low[0] = (r.back_turned[...] * (HD ** -0.5)).astype(BF)
+    r.back_heads[head] = r.back_low[0]
     out_cross.wait_recv()
     turned = r.out_heads[...].reshape(128, 512)
     r.pair_out[...] = turned
@@ -1029,25 +1037,12 @@
         r.out_cols[j] = out_grad[:, 128 * j : 128 * j + 128]
     out_cols = trade_t(wire, place, r.out_cols, r.out_in)
     r.out_in[t] = r.out_cols[t]
-    columns = (far, cross, mate, x)
-    for step, column in enumerate(columns):
-        backward_column(r, place, column, diagonal=step == 3)
-        dk_swap.append(wire.push(r.dk.at[1 - c, column], r.dk_in.at[column], sibling))
-        if step > 0:
-            send_column(step - 1, columns[step - 1])
-    r.back_low[0] = (r.back_turned[...] * (HD ** -0.5)).astype(BF)
-    r.back_heads[head] = r.back_low[0]
     arrive(gf_z)
     r.gf_line[...] = total(r.gf_chip[z], r.gf_z).astype(BF)
     gf_x = []
     for k in range(1, 4):
         goal = ring(x, k)
         gf_x.append(wire.push(r.gf_line.at[goal], r.gf_x.at[k - 1], place.at(x=goal)))
-    arrive(out_cols)
-    for j in range(4):
-        by_owner(r.go, j, r.out_in[j], 0, 128)
-    go_swap = sum_cores(wire, place, r.go, r.go_core)
-
     def feed_out(i, _):
         blocks = pl.ds(2 * i, 2)
         part = r.hidden[blocks].reshape(256, 512)
@@ -1057,10 +1052,6 @@
         return 0
 
     lax.fori_loop(0, 2, feed_out, 0)
-    go_swap.wait_recv()
-    for a in range(4):
-        r.go_chip[a] = (r.go[c, a].astype(F32) + r.go_core[a].astype(F32)).astype(BF)
-    go_all = scatter_plane(wire, place, r.go_chip, r.go_in)
     out_rows = r.w_output[pl.ds(8 * t, 8)].reshape(128, 512)
     for i in range(2):
         blocks, lanes = slice(2 * i, 2 * i + 2), slice(256 * i, 256 * i + 256)
@@ -1073,6 +1064,11 @@
     cosine, sine = r.cos[...].reshape(512, 128), r.sin[...].reshape(512, 128)
     r.joint_out[:, 0:128] = turn(back, cosine, sine, -1.0).astype(BF)
     low = lax.broadcasted_iota(jnp.int32, (128, 128), 1) < 64
+    arrive(out_cols)
+    for j in range(4):
+        by_owner(r.go, j, r.out_in[j], 0, 128)
+    go_swap = sum_cores(wire, place, r.go, r.go_core)
+
     arrive([dk_swap[3], *dk_sent])
     r.dkv[head] = (chip_sum(x) + r.dk_got[2].astype(F32)).astype(BF)
     r.dkv[1 - head] = (r.dk_got[0].astype(F32) + r.dk_got[1].astype(F32)).astype(BF)
@@ -1088,6 +1084,10 @@
         part = r.normed[:, :, 128 * j : 128 * j + 128].reshape(512, 128)
         by_owner(r.gj, j, dot_rows(part, r.joint_out[...]).astype(BF), 0, 384)
     gj_swap = sum_cores(wire, place, r.gj, r.gj_core)
+    go_swap.wait_recv()
+    for a in range(4):
+        r.go_chip[a] = (r.go[c, a].astype(F32) + r.go_core[a].astype(F32)).astype(BF)
+    go_all = scatter_plane(wire, place, r.go_chip, r.go_in)
 
     r.vp[0] = jnp.zeros((4, 16, 128), F32)
     shift_sum = jnp.zeros((1, 512), F32)

time: 101 us -> 101 us (level)
  no operation moved by 1% of the time
where the time goes in v3:
time: 101 us; the launch traced here: 100 us
  Pallas kernels  99.6 us (99%)
    pallas_call x1, Pallas kernels, block_stage(): pl.pallas_call(block_kernel, out_shape=tuple((shape(dims, dtype) for _, d...  97.4 us
    pallas_call x1, Pallas kernels, write_stage(): pl.pallas_call(write_kernel, out_shape=tuple((shape(a.shape, a.dtype) for...  2.22 us

profile of v3, /device:TPU:1, one launch (start us, length us, event | category | flops | bytes accessed | tf_op | source)
XLA Modules:
  0.0 100.5 jit_solution(3645433620343302626)
XLA Ops:
  0.7 97.4 %block.1 = (f32[4,1536]{1,0:T(4,128)}, f32[4,512]{1,0:T(4,128)}, f32[4,2048]{1,0:T(4,128)}, f32[4,2048]{1,0:T(4,128)}, f32[4,1536]{1,0:T(4,128)}, /*index=5*/f32...) custom-call(s32[1,4]{1,0:T(1,128)} %refs_0_.1, ...), custom_call_target="tpu_custom_call" | custom-call | tf_op jit(solution)/shard_map/block/pallas_call | solution.py:1359
  98.1 2.2 %write.1 = (f32[4,1536]{1,0:T(4,128)}, f32[4,512]{1,0:T(4,128)}, f32[4,2048]{1,0:T(4,128)}, f32[4,2048]{1,0:T(4,128)}, f32[4,1536]{1,0:T(4,128)}, /*index=5*/f32...) custom-call(f32[4,1536]{1,0:T(4,128)} %get-tuple-element.51.refs_0_,, ...), custom_call_target="tpu_custom_call" | custom-call | tf_op jit(solution)/shard_map/write/pallas_call | solution.py:1391
